TPU v7x, 256 devices: a whole 4x4x8 slice. The times are simulated.
256 devices in a mesh: dp: 2 (over core), head: 8 (over x, z_lo), ctx: 16 (over y, z_hi).
Axes of the slice: x: 4, y: 4, z: 8 (z_hi: 4, z_lo: 2; z = z_hi * 2 + z_lo), core: 2. Of those that a mesh axis runs over, the one named last changes fastest.
Arguments:
- query_states: bfloat16 [2, 16384, 32, 128], P('dp', 'ctx', 'head'), may hold values from -6 to 6
- key_states: bfloat16 [2, 16384, 8, 128], P('dp', 'ctx', 'head'), may hold values from -6 to 6
- value_states: bfloat16 [2, 16384, 8, 128], P('dp', 'ctx', 'head'), may hold values from -12 to 12
- gate_values: float32 [32], P('head'), may hold values from 0.1 to 0.9
- head_flags: int32 [32], P('head'), may hold values from 0 to 1, as said below
- output_grad: bfloat16 [2, 16384, 32, 128], P('dp', 'ctx', 'head'), may hold values from -16 to 16
Outputs:
- blended: bfloat16 [2, 16384, 32, 128], P('dp', 'ctx', 'head')
- gate_grad: float32 [32], replicated
Inputs may be any that keep to these rules, and one draw needn't show every extreme that they name: `head_flags`: exactly 1 of the 4 query heads of each key-value head have flag 1.
All inputs are finite; a program needn't handle non-finite values.
Results may differ from a plain program's by a relative error of at most 0.005.
Values may be sent and summed in bfloat16 or wider, within the bound.
No kernel may reach another device: no remote copies, remote signals or barrier semaphores. Data moves between devices by JAX's collectives and lax.ppermute only.
A program may use at most 64 MiB of HBM per device.

v0:
```python
import math
import jax
import jax.numpy as jnp
from jax import lax
from jax.sharding import PartitionSpec as P

RET = 1
SINK = 64
WINDOW = 2048


def from_behind(block, axis, distance):
    devices = range(lax.axis_size(axis))
    route = [(i - distance, i) for i in devices if i - distance in devices]
    return lax.ppermute(block, axis, route)


def empty_state(row_count, groups, heads, width):
    return (
        jnp.full((row_count, groups, heads), -jnp.inf, jnp.float32),
        jnp.zeros((row_count, groups, heads), jnp.float32),
        jnp.zeros((row_count, groups, heads, width), jnp.float32),
    )


def block_update(carried, query_block, key_rows, value_rows, allowed):
    running_max, running_sum, running_acc = carried
    scaling = 1.0 / math.sqrt(query_block.shape[-1])
    scores = (
        jnp.einsum("rgeh,kgh->rgek", query_block, key_rows, preferred_element_type=jnp.float32)
        * scaling
    )
    visible = allowed[:, None, None, :]
    scores = jnp.where(visible, scores, -jnp.inf)
    newest = jnp.maximum(running_max, jnp.max(scores, axis=-1))
    anchor = jnp.where(newest == -jnp.inf, 0.0, newest)
    factor = jnp.exp(running_max - anchor)
    weights = jnp.where(visible, jnp.exp(scores - anchor[..., None]), 0.0)
    running_sum = running_sum * factor + jnp.sum(weights, axis=-1)
    update = jnp.einsum(
        "rgek,kgh->rgeh",
        weights.astype(jnp.bfloat16),
        value_rows,
        preferred_element_type=jnp.float32,
    )
    running_acc = running_acc * factor[..., None] + update
    return (newest, running_sum, running_acc)


def sweep_blocks(carried, queries, positions, key_rows, value_rows, key_first, needed, allowed_fn):
    row_count = queries.shape[0]
    key_count = key_rows.shape[0]
    row_block = math.gcd(row_count, 512)
    key_block = math.gcd(key_count, 512)
    key_steps = key_count // key_block
    total_steps = row_count // row_block * key_steps

    def visit_block(counter, current):
        row_at = counter // key_steps * row_block
        key_at = counter % key_steps * key_block
        row_pos = lax.dynamic_slice_in_dim(positions, row_at, row_block)
        key_pos = key_first + key_at + jnp.arange(key_block, dtype=jnp.int32)

        def compute(present):
            portion = tuple(
                (lax.dynamic_slice_in_dim(member, row_at, row_block) for member in present)
            )
            renewed = block_update(
                portion,
                lax.dynamic_slice_in_dim(queries, row_at, row_block),
                lax.dynamic_slice_in_dim(key_rows, key_at, key_block),
                lax.dynamic_slice_in_dim(value_rows, key_at, key_block),
                allowed_fn(row_pos[:, None], key_pos[None, :]),
            )
            return tuple(
                (
                    lax.dynamic_update_slice_in_dim(member, fresh_part, row_at, 0)
                    for member, fresh_part in zip(present, renewed)
                )
            )

        def unchanged(present):
            return present

        return lax.cond(
            needed(row_pos[0], row_pos[row_block - 1], key_pos[0], key_pos[key_block - 1]),
            compute,
            unchanged,
            current,
        )

    return lax.fori_loop(0, total_steps, visit_block, carried)


def causal_needed(row_low, row_high, key_low, key_high):
    return key_low <= row_high


def causal_allowed(row_pos, key_pos):
    return key_pos <= row_pos


def window_needed(row_low, row_high, key_low, key_high):
    return (key_low <= row_high) & (key_high > row_low - WINDOW)


def window_allowed(row_pos, key_pos):
    return (key_pos >= 0) & (key_pos <= row_pos) & (row_pos - key_pos < WINDOW)


def sinks_needed(row_low, row_high, key_low, key_high):
    return (key_low < SINK) & (row_high - key_low >= WINDOW)


def sinks_allowed(row_pos, key_pos):
    return (key_pos < SINK) & (key_pos <= row_pos) & (row_pos - key_pos >= WINDOW)


def on_device(query_states, key_states, value_states, gate_values, head_flags, output_grad):
    tok_rows = query_states.shape[1]
    groups = key_states.shape[2]
    head_dim = key_states.shape[3]
    per_group = query_states.shape[2] // groups
    ctx_count = lax.axis_size("ctx")
    ctx_index = lax.axis_index("ctx")
    queries = query_states[0].reshape(tok_rows, groups, per_group, head_dim)
    stacked = jnp.stack([key_states[0], value_states[0]])
    marked = head_flags.reshape(groups, per_group)
    ordinal = jnp.cumsum(marked, axis=1) - 1
    slot_ids = jnp.arange(RET, dtype=jnp.int32)
    picker = ((marked[:, None, :] == 1) & (ordinal[:, None, :] == slot_ids[None, :, None])).astype(
        jnp.float32
    )
    chosen = jnp.einsum(
        "gre,tgeh->tgrh", picker.astype(jnp.bfloat16), queries, preferred_element_type=jnp.float32
    ).astype(jnp.bfloat16)
    own_pos = ctx_index * tok_rows + jnp.arange(tok_rows, dtype=jnp.int32)
    full_state = empty_state(tok_rows, groups, RET, head_dim)
    near_state = empty_state(tok_rows, groups, per_group, head_dim)
    portion = lax.all_gather(stacked, "ctx", axis=1, tiled=True)
    start = jnp.int32(0)
    full_now = sweep_blocks(
        full_state, chosen, own_pos, portion[0], portion[1], start, causal_needed, causal_allowed
    )
    head_rows = min(SINK, portion.shape[1])
    sink_part = portion[:, :head_rows]

    def with_sinks(present):
        return sweep_blocks(
            present,
            queries,
            own_pos,
            sink_part[0],
            sink_part[1],
            start,
            sinks_needed,
            sinks_allowed,
        )

    def without_sinks(present):
        return present

    near_now = lax.cond(start < SINK, with_sinks, without_sinks, near_state)
    near_state = near_now
    reach_depth = min((WINDOW - 1) // tok_rows + 1, ctx_count - 1)
    earlier = [from_behind(stacked, "ctx", distance) for distance in range(reach_depth, 0, -1)]
    near_keys = jnp.concatenate(earlier + [stacked], axis=1)
    near_state = sweep_blocks(
        near_state,
        queries,
        own_pos,
        near_keys[0],
        near_keys[1],
        (ctx_index - reach_depth) * tok_rows,
        window_needed,
        window_allowed,
    )
    full_out = full_now[2] / full_now[1][..., None]
    near_out = near_state[2] / near_state[1][..., None]
    full_heads = jnp.einsum("gre,tgrh->tgeh", picker, full_out, precision=lax.Precision.HIGHEST)
    gate_cols = gate_values.reshape(groups, per_group)[None, :, :, None]
    retrieval = (marked == 1)[None, :, :, None]
    mixed = jnp.where(retrieval, gate_cols * full_heads + (1.0 - gate_cols) * near_out, near_out)
    blended = mixed.astype(jnp.bfloat16).reshape(1, tok_rows, groups * per_group, head_dim)
    grad_rows = output_grad[0].reshape(tok_rows, groups, per_group, head_dim).astype(jnp.float32)
    local_terms = jnp.sum(grad_rows * (full_heads - near_out), axis=(0, 3)) * marked.astype(
        jnp.float32
    )
    heads_dev = groups * per_group
    padded = lax.dynamic_update_slice_in_dim(
        jnp.zeros((heads_dev * lax.axis_size("head"),), jnp.float32),
        local_terms.reshape(heads_dev),
        lax.axis_index("head") * heads_dev,
        0,
    )
    totals = lax.psum(padded, ("dp", "head", "ctx"))
    normalizer = 1.0 / math.sqrt(
        lax.axis_size("dp") * query_states.shape[0] * tok_rows * ctx_count * head_dim
    )
    return (blended, totals * normalizer)


def solution(mesh):
    return jax.shard_map(
        on_device,
        mesh=mesh,
        in_specs=(
            P("dp", "ctx", "head", None),
            P("dp", "ctx", "head", None),
            P("dp", "ctx", "head", None),
            P("head"),
            P("head"),
            P("dp", "ctx", "head", None),
        ),
        out_specs=(P("dp", "ctx", "head", None), P()),
        check_vma=False,
    )
```

profile of v0, /device:TPU:1, one launch (start us, length us, event | category | flops | bytes accessed | tf_op | source)
XLA Modules:
  0.0 829.5 jit_solution(2054756737701288816)
XLA Ops:
  10.1 5.8 collective-permute-start.1
  15.9 7.8 collective-permute-start
  31.2 24.1 %collective-permute-done = bf16[2,1024,1,128]{3,1,2,0:T(8,128)(2,1)} collective-permute-done((bf16[2,1024,1,128]{3,1,2,0:T(8,128)(2,1)}, bf16[2,1024,1,128]{3,1,2,0:T(8,128)(2,1)}, u32[]{:S(2)}, u32[]{:S(2)}) %collective-permute-start) | collective-permute-done | bytes 524320 | tf_op jit(solution)/shard_map/ppermute | solution.py:15
  58.6 96.1 %all-gather.2.cloned.1.call-done = bf16[2,16384,1,128]{3,1,2,0:T(8,128)(2,1)} async-done(((bf16[2,1024,1,128]{3,1,2,0:T(8,128)(2,1)}), bf16[2,16384,1,128]{3,1,2,0:T(8,128)(2,1)}) %all-gather.2.cloned.1.call-update) | async-done | bytes 8388624 | tf_op jit(solution)/shard_map/all_gather | solution.py:140
  154.6 5.7 slice_bitcast_fusion
  160.4 183.1 %while.58 = (s32[]{:T(128)}, f32[1024,1,1]{0,2,1:T(1,128)S(1)}, f32[1024,1,1]{0,2,1:T(1,128)S(1)}, f32[1024,1,1,128]{0,3,2,1:T(8,128)S(1)}, s32[1024]{0:T(1024)S...) while((s32[]{:T(128)}, f32[1024,1,1]{0,2,1:T(1,128)S(1)}, ...), condition=%wide.region_6.7_spmd, body=%wide.region_1.6_spmd.sunk | while | flops 137498128 | bytes 4645472 | solution.py:92
  350.4 158.5 %while.60 = (s32[]{:T(128)}, f32[1024,1,4]{0,2,1:T(4,128)S(1)}, f32[1024,1,4]{0,2,1:T(4,128)S(1)}, f32[1024,1,4,128]{0,3,2,1:T(8,128)}, s32[]{:T(128)}, /*index=...) while((s32[]{:T(128)}, f32[1024,1,4]{0,2,1:T(4,128)S(1)}, ...), condition=%wide.region_18.19_spmd, body=%wide.region_13.18_spmd.sunk | while | flops 552356864 | bytes 27178672 | solution.py:92
  353.4 12.6 %conditional.8 = ((f32[1024,1,4]{0,2,1:T(4,128)S(1)}, f32[1024,1,4]{0,2,1:T(4,128)S(1)}, f32[1024,1,4,128]{0,3,2,1:T(8,128)})) conditional(s32[]{:T(128)} %bitcast.205, (f32[1024,1,4]{0,2,1:T(4,128)S(1)}, f32[1024,1,4]{0,2,1:T(4,128)S(1)}, f32[1024,1,4,128]{0,3,2,1:T(8,128)}) %tuple.164, (s32[]{:T(128)}, f32[1024,1,4]{0,2,1:T(4,128)S(1)}, ...), branch_computations={%region_14.14_spmd, %region_15.17_spmd} | conditional | flops 552356352 | bytes 27172004 | solution.py:85
  360.3 5.7 dynamic_update_slice.31
  369.1 12.6 %conditional.8 = ((f32[1024,1,4]{0,2,1:T(4,128)S(1)}, f32[1024,1,4]{0,2,1:T(4,128)S(1)}, f32[1024,1,4,128]{0,3,2,1:T(8,128)})) conditional(s32[]{:T(128)} %bitcast.205, (f32[1024,1,4]{0,2,1:T(4,128)S(1)}, f32[1024,1,4]{0,2,1:T(4,128)S(1)}, f32[1024,1,4,128]{0,3,2,1:T(8,128)}) %tuple.164, (s32[]{:T(128)}, f32[1024,1,4]{0,2,1:T(4,128)S(1)}, ...), branch_computations={%region_14.14_spmd, %region_15.17_spmd} | conditional | flops 552356352 | bytes 27172004 | solution.py:85
  376.0 5.7 dynamic_update_slice.31
  384.8 12.6 %conditional.8 = ((f32[1024,1,4]{0,2,1:T(4,128)S(1)}, f32[1024,1,4]{0,2,1:T(4,128)S(1)}, f32[1024,1,4,128]{0,3,2,1:T(8,128)})) conditional(s32[]{:T(128)} %bitcast.205, (f32[1024,1,4]{0,2,1:T(4,128)S(1)}, f32[1024,1,4]{0,2,1:T(4,128)S(1)}, f32[1024,1,4,128]{0,3,2,1:T(8,128)}) %tuple.164, (s32[]{:T(128)}, f32[1024,1,4]{0,2,1:T(4,128)S(1)}, ...), branch_computations={%region_14.14_spmd, %region_15.17_spmd} | conditional | flops 552356352 | bytes 27172004 | solution.py:85
  391.6 5.7 dynamic_update_slice.31
  400.4 12.6 %conditional.8 = ((f32[1024,1,4]{0,2,1:T(4,128)S(1)}, f32[1024,1,4]{0,2,1:T(4,128)S(1)}, f32[1024,1,4,128]{0,3,2,1:T(8,128)})) conditional(s32[]{:T(128)} %bitcast.205, (f32[1024,1,4]{0,2,1:T(4,128)S(1)}, f32[1024,1,4]{0,2,1:T(4,128)S(1)}, f32[1024,1,4,128]{0,3,2,1:T(8,128)}) %tuple.164, (s32[]{:T(128)}, f32[1024,1,4]{0,2,1:T(4,128)S(1)}, ...), branch_computations={%region_14.14_spmd, %region_15.17_spmd} | conditional | flops 552356352 | bytes 27172004 | solution.py:85
  407.3 5.7 dynamic_update_slice.31
  416.1 12.6 %conditional.8 = ((f32[1024,1,4]{0,2,1:T(4,128)S(1)}, f32[1024,1,4]{0,2,1:T(4,128)S(1)}, f32[1024,1,4,128]{0,3,2,1:T(8,128)})) conditional(s32[]{:T(128)} %bitcast.205, (f32[1024,1,4]{0,2,1:T(4,128)S(1)}, f32[1024,1,4]{0,2,1:T(4,128)S(1)}, f32[1024,1,4,128]{0,3,2,1:T(8,128)}) %tuple.164, (s32[]{:T(128)}, f32[1024,1,4]{0,2,1:T(4,128)S(1)}, ...), branch_computations={%region_14.14_spmd, %region_15.17_spmd} | conditional | flops 552356352 | bytes 27172004 | solution.py:85
  423.0 5.7 dynamic_update_slice.31
  438.0 11.7 %conditional.8 = ((f32[1024,1,4]{0,2,1:T(4,128)S(1)}, f32[1024,1,4]{0,2,1:T(4,128)S(1)}, f32[1024,1,4,128]{0,3,2,1:T(8,128)})) conditional(s32[]{:T(128)} %bitcast.205, (f32[1024,1,4]{0,2,1:T(4,128)S(1)}, f32[1024,1,4]{0,2,1:T(4,128)S(1)}, f32[1024,1,4,128]{0,3,2,1:T(8,128)}) %tuple.164, (s32[]{:T(128)}, f32[1024,1,4]{0,2,1:T(4,128)S(1)}, ...), branch_computations={%region_14.14_spmd, %region_15.17_spmd} | conditional | flops 552356352 | bytes 27172004 | solution.py:85
  452.8 11.8 %conditional.8 = ((f32[1024,1,4]{0,2,1:T(4,128)S(1)}, f32[1024,1,4]{0,2,1:T(4,128)S(1)}, f32[1024,1,4,128]{0,3,2,1:T(8,128)})) conditional(s32[]{:T(128)} %bitcast.205, (f32[1024,1,4]{0,2,1:T(4,128)S(1)}, f32[1024,1,4]{0,2,1:T(4,128)S(1)}, f32[1024,1,4,128]{0,3,2,1:T(8,128)}) %tuple.164, (s32[]{:T(128)}, f32[1024,1,4]{0,2,1:T(4,128)S(1)}, ...), branch_computations={%region_14.14_spmd, %region_15.17_spmd} | conditional | flops 552356352 | bytes 27172004 | solution.py:85
  467.6 11.7 %conditional.8 = ((f32[1024,1,4]{0,2,1:T(4,128)S(1)}, f32[1024,1,4]{0,2,1:T(4,128)S(1)}, f32[1024,1,4,128]{0,3,2,1:T(8,128)})) conditional(s32[]{:T(128)} %bitcast.205, (f32[1024,1,4]{0,2,1:T(4,128)S(1)}, f32[1024,1,4]{0,2,1:T(4,128)S(1)}, f32[1024,1,4,128]{0,3,2,1:T(8,128)}) %tuple.164, (s32[]{:T(128)}, f32[1024,1,4]{0,2,1:T(4,128)S(1)}, ...), branch_computations={%region_14.14_spmd, %region_15.17_spmd} | conditional | flops 552356352 | bytes 27172004 | solution.py:85
  482.4 11.8 %conditional.8 = ((f32[1024,1,4]{0,2,1:T(4,128)S(1)}, f32[1024,1,4]{0,2,1:T(4,128)S(1)}, f32[1024,1,4,128]{0,3,2,1:T(8,128)})) conditional(s32[]{:T(128)} %bitcast.205, (f32[1024,1,4]{0,2,1:T(4,128)S(1)}, f32[1024,1,4]{0,2,1:T(4,128)S(1)}, f32[1024,1,4,128]{0,3,2,1:T(8,128)}) %tuple.164, (s32[]{:T(128)}, f32[1024,1,4]{0,2,1:T(4,128)S(1)}, ...), branch_computations={%region_14.14_spmd, %region_15.17_spmd} | conditional | flops 552356352 | bytes 27172004 | solution.py:85
  497.2 11.7 %conditional.8 = ((f32[1024,1,4]{0,2,1:T(4,128)S(1)}, f32[1024,1,4]{0,2,1:T(4,128)S(1)}, f32[1024,1,4,128]{0,3,2,1:T(8,128)})) conditional(s32[]{:T(128)} %bitcast.205, (f32[1024,1,4]{0,2,1:T(4,128)S(1)}, f32[1024,1,4]{0,2,1:T(4,128)S(1)}, f32[1024,1,4,128]{0,3,2,1:T(8,128)}) %tuple.164, (s32[]{:T(128)}, f32[1024,1,4]{0,2,1:T(4,128)S(1)}, ...), branch_computations={%region_14.14_spmd, %region_15.17_spmd} | conditional | flops 552356352 | bytes 27172004 | solution.py:85
  511.2 6.3 fusion.69
  517.7 304.5 %psum.7 = f32[32]{0:T(128)S(1)} all-reduce(f32[32]{0:T(128)S(1)} %multiply_dynamic-update-slice_fusion), channel_id=1, replica_groups=mesh['dp'=2,'head'=8,'ctx'=16] {'dp','head','ctx'}, use_global_device_ids=true, to_apply=%region_20.21 | all-reduce | flops 32 | bytes 256 | tf_op jit(solution)/shard_map/psum | solution.py:196
  (560 shorter events, 232.3 us)
Async XLA Ops:
  7.2 20.2 %copy-start.4 = (bf16[1,1024,4,128]{3,2,1,0:T(4,128)(2,1)S(1)}, bf16[1,1024,4,128]{3,2,1,0:T(4,128)(2,1)}, u32[]{:S(2)}) copy-start(bf16[1,1024,4,128]{3,2,1,0:T(4,128)(2,1)} %param.18) | copy-start | bytes 3145732
  7.2 147.5 %all-gather.2.cloned.1.call-start = ((), (), s32[]{:S(2)}) async-start(), calls=%async_computation | async-start | bytes 8912896 | tf_op jit(solution)/shard_map/all_gather | solution.py:140
  9.3 0.8 copy-start.1
  10.1 21.1 %collective-permute-start.1 = (bf16[2,1024,1,128]{3,1,2,0:T(8,128)(2,1)}, bf16[2,1024,1,128]{3,1,2,0:T(8,128)(2,1)S(1)}, u32[]{:S(2)}, u32[]{:S(2)}) collective-permute-start(bf16[2,1024,1,128]{3,1,2,0:T(8,128)(2,1)} %copy-done.1), channel_id=1, source_target_pairs={{0,1},{1,2},{2,3},{3,4},{4,5},{5,6},{6,7},{7,8},{8,9},{9,10},{10,1... | collective-permute-start | bytes 1572872 | tf_op jit(solution)/shard_map/ppermute | solution.py:15
  15.9 39.4 %collective-permute-start = (bf16[2,1024,1,128]{3,1,2,0:T(8,128)(2,1)}, bf16[2,1024,1,128]{3,1,2,0:T(8,128)(2,1)}, u32[]{:S(2)}, u32[]{:S(2)}) collective-permute-start(bf16[2,1024,1,128]{3,1,2,0:T(8,128)(2,1)} %copy-done.1), channel_id=1, source_target_pairs={{0,2},{1,3},{2,4},{3,5},{4,6},{5,7},{6,8},{7,9},{8,10},{9,11},{10,... | collective-permute-start | bytes 1572872 | tf_op jit(solution)/shard_map/ppermute | solution.py:15
  25.8 29.4 %copy-start.2 = (bf16[2,1024,1,128]{3,1,2,0:T(8,128)(2,1)S(1)}, bf16[2,1024,1,128]{3,1,2,0:T(8,128)(2,1)}, u32[]{:S(2)}) copy-start(bf16[2,1024,1,128]{3,1,2,0:T(8,128)(2,1)} %copy-done.1) | copy-start | bytes 1572868
  355.7 1.6 copy-start
  371.4 1.6 copy-start
  387.0 1.6 copy-start
  402.7 1.6 copy-start
  418.4 1.6 copy-start
  440.3 1.6 copy-start
  455.1 1.6 copy-start
  469.9 1.6 copy-start
  484.7 1.6 copy-start
  499.5 1.6 copy-start
  508.9 2.3 copy-start.3
  508.9 2.3 copy-start.6
  511.2 6.4 copy-start.5
Sparse Core Ops, SparseCore 0:
  10.5 144.0 all-gather.1
where the time goes:
time: 836 us; the launch traced here: 829 us
  blocking collectives  304 us (36%)
  local copies, waits for them, and re-layouts  177 us (21%)
  waiting for transfers between devices  123 us (15%)
  loops' own time  119 us (14%)
  matrix products  50 us (6%)
  other arithmetic  27.9 us (3%)
  between operations  14.2 us (2%)
  starting transfers between devices  13.6 us (2%)
    psum x1, blocking collectives, on_device(): totals = lax.psum(padded, ('dp', 'head', 'ctx'))  304 us
    another operation x3, loops' own time, sweep_blocks(): return lax.fori_loop(0, total_steps, visit_block, carried)  117 us
    all_gather x1, waiting for transfers between devices, on_device(): portion = lax.all_gather(stacked, 'ctx', axis=1, tiled=True)  96.1 us
    dynamic_update_slice x39, local copies, waits for them, and re-layouts, compute(): lax.dynamic_update_slice_in_dim(member, fresh_part, row_at, 0)  60.7 us
    slice x66, local copies, waits for them, and re-layouts, visit_block(): row_pos[row_block - 1]  42.8 us
    slice x64, local copies, waits for them, and re-layouts, visit_block(): key_pos[0]  37.7 us
    ppermute x2, waiting for transfers between devices, from_behind(): return lax.ppermute(block, axis, route)  27.2 us
    dot_general x13, matrix products, block_update(): jnp.einsum('rgek,kgh->rgeh', weights.astype(jnp.bfloat16), value_rows, pr...  26.8 us
  transfers between devices with their start and end apart: 3, of which 3 were waited for; matrix products, arithmetic and copies ran while one was open for 1% of the time, Pallas kernels for 0%

commit v1 on v0

--- a/solution.py
+++ b/solution.py
@@ -137,7 +137,9 @@
     own_pos = ctx_index * tok_rows + jnp.arange(tok_rows, dtype=jnp.int32)
     full_state = empty_state(tok_rows, groups, RET, head_dim)
     near_state = empty_state(tok_rows, groups, per_group, head_dim)
-    portion = lax.all_gather(stacked, "ctx", axis=1, tiled=True)
+    portion = jnp.concatenate(
+        lax.all_to_all(jnp.stack([stacked] * lax.axis_size("ctx")), "ctx", 0, 0), axis=1
+    )
     start = jnp.int32(0)
     full_now = sweep_blocks(
         full_state, chosen, own_pos, portion[0], portion[1], start, causal_needed, causal_allowed

time: 836 us -> 952 us (1.14)
  waiting for transfers between devices: 123 us -> 212 us
  local copies, waits for them, and re-layouts: 177 us -> 198 us
  matrix products: 50 us -> 66.2 us
  between operations: 14.2 us -> 0.78 us
    ppermute x2, waiting for transfers between devices: 27.2 us -> 212 us  [from_behind(): return lax.ppermute(block, axis, route)]
    all_gather x1 -> x0, waiting for transfers between devices: 96.1 us -> none  [on_device(): portion = lax.all_gather(stacked, 'ctx', axis=1, tiled=True)]
    dot_general x13, matrix products: 26.8 us -> 43.2 us  [block_update(): jnp.einsum('rgek,kgh->rgeh', weights.astype(jnp.bfloat16), value_rows, pr...]
    cond x20, local copies, waits for them, and re-layouts: 4.34 us -> 18.2 us
    all_to_all x0 -> x1, starting transfers between devices: none -> 11.9 us  [on_device(): lax.all_to_all(jnp.stack([stacked] * lax.axis_size('ctx')), 'ctx', 0, 0)]
  transfers between devices with their start and end apart: 3 -> 3, of which waited for: 3 -> 2; matrix products, arithmetic and copies ran while one was open for 1% -> 0% of each run, Pallas kernels for 0% -> 0%
where the time goes in v1:
time: 952 us; the launch traced here: 946 us
  blocking collectives  304 us (32%)
  waiting for transfers between devices  212 us (22%)
  local copies, waits for them, and re-layouts  198 us (21%)
  loops' own time  116 us (12%)
  matrix products  66.2 us (7%)
  other arithmetic  25.9 us (3%)
  starting transfers between devices  22.1 us (2%)
    psum x1, blocking collectives, on_device(): totals = lax.psum(padded, ('dp', 'head', 'ctx'))  304 us
    ppermute x2, waiting for transfers between devices, from_behind(): return lax.ppermute(block, axis, route)  212 us
    another operation x3, loops' own time, sweep_blocks(): return lax.fori_loop(0, total_steps, visit_block, carried)  115 us
    dynamic_update_slice x39, local copies, waits for them, and re-layouts, compute(): lax.dynamic_update_slice_in_dim(member, fresh_part, row_at, 0)  61 us
    dot_general x13, matrix products, block_update(): jnp.einsum('rgek,kgh->rgeh', weights.astype(jnp.bfloat16), value_rows, pr...  43.2 us
    slice x66, local copies, waits for them, and re-layouts, visit_block(): row_pos[row_block - 1]  38.7 us
    slice x64, local copies, waits for them, and re-layouts, visit_block(): key_pos[0]  37.6 us
    dot_general x13, matrix products, block_update(): jnp.einsum('rgeh,kgh->rgek', query_block, key_rows, preferred_element_typ...  22.4 us
  transfers between devices with their start and end apart: 3, of which 2 were waited for; matrix products, arithmetic and copies ran while one was open for 0% of the time, Pallas kernels for 0%

profile of v1, /device:TPU:1, one launch (start us, length us, event | category | flops | bytes accessed | tf_op | source)
XLA Modules:
  0.0 946.3 jit_solution(4450319516738055069)
XLA Ops:
  7.7 11.9 %all-to-all-start = ((bf16[16,2,1024,1,128]{4,2,3,1,0:T(8,128)(2,1)}), bf16[16,2,1024,1,128]{4,2,3,1,0:T(8,128)(2,1)}, u32[]{:S(2)}, u32[]{:S(2)}) async-start(bf16[16,2,1024,1,128]{4,2,3,1,0:T(8,128)(2,1)} %stack.8), calls=%async_computation | async-start | bytes 16777216 | tf_op jit(solution)/shard_map/all_to_all | solution.py:141
  23.8 6.0 collective-permute-start
  30.9 190.5 %collective-permute-done.1 = bf16[2,1024,1,128]{3,1,2,0:T(8,128)(2,1)S(1)} collective-permute-done((bf16[2,1024,1,128]{3,1,2,0:T(8,128)(2,1)S(1)}, bf16[2,1024,1,128]{3,1,2,0:T(8,128)(2,1)S(1)}, u32[]{:S(2)}, u32[]{:S(2)}) %collective-permute-start.1) | collective-permute-done | bytes 524320 | tf_op jit(solution)/shard_map/ppermute | solution.py:15
  221.4 21.8 %collective-permute-done = bf16[2,1024,1,128]{3,1,2,0:T(8,128)(2,1)} collective-permute-done((bf16[2,1024,1,128]{3,1,2,0:T(8,128)(2,1)S(1)}, bf16[2,1024,1,128]{3,1,2,0:T(8,128)(2,1)}, u32[]{:S(2)}, u32[]{:S(2)}) %collective-permute-start) | collective-permute-done | bytes 524320 | tf_op jit(solution)/shard_map/ppermute | solution.py:15
  246.5 7.5 copy.41
  254.0 5.8 fusion.83
  259.9 174.4 %while.58 = (s32[]{:T(128)}, f32[1024,1,1]{0,2,1:T(1,128)S(1)}, f32[1024,1,1]{0,2,1:T(1,128)S(1)}, f32[1024,1,1,128]{0,3,2,1:T(8,128)S(1)}, s32[1024]{0:T(1024)S...) while((s32[]{:T(128)}, f32[1024,1,1]{0,2,1:T(1,128)S(1)}, ...), condition=%wide.region_6.7_spmd, body=%wide.region_1.6_spmd.sunk | while | flops 137498128 | bytes 4645472 | solution.py:92
  440.9 191.8 %while.60 = (s32[]{:T(128)}, f32[1024,1,4]{0,2,1:T(4,128)S(1)}, f32[1024,1,4]{0,2,1:T(4,128)S(1)}, f32[1024,1,4,128]{0,3,2,1:T(8,128)}, s32[]{:T(128)}, /*index=...) while((s32[]{:T(128)}, f32[1024,1,4]{0,2,1:T(4,128)S(1)}, ...), condition=%wide.region_18.19_spmd, body=%wide.region_13.18_spmd.sunk | while | flops 552356864 | bytes 35567280 | solution.py:92
  444.2 15.7 %conditional.8 = ((f32[1024,1,4]{0,2,1:T(4,128)S(1)}, f32[1024,1,4]{0,2,1:T(4,128)S(1)}, f32[1024,1,4,128]{0,3,2,1:T(8,128)})) conditional(s32[]{:T(128)} %bitcast.211, (f32[1024,1,4]{0,2,1:T(4,128)S(1)}, f32[1024,1,4]{0,2,1:T(4,128)S(1)}, f32[1024,1,4,128]{0,3,2,1:T(8,128)}) %tuple.165, (s32[]{:T(128)}, f32[1024,1,4]{0,2,1:T(4,128)S(1)}, ...), branch_computations={%region_14.14_spmd, %region_15.17_spmd} | conditional | flops 552356352 | bytes 35560612 | solution.py:85
  454.1 5.8 dynamic_update_slice.31
  463.2 15.7 %conditional.8 = ((f32[1024,1,4]{0,2,1:T(4,128)S(1)}, f32[1024,1,4]{0,2,1:T(4,128)S(1)}, f32[1024,1,4,128]{0,3,2,1:T(8,128)})) conditional(s32[]{:T(128)} %bitcast.211, (f32[1024,1,4]{0,2,1:T(4,128)S(1)}, f32[1024,1,4]{0,2,1:T(4,128)S(1)}, f32[1024,1,4,128]{0,3,2,1:T(8,128)}) %tuple.165, (s32[]{:T(128)}, f32[1024,1,4]{0,2,1:T(4,128)S(1)}, ...), branch_computations={%region_14.14_spmd, %region_15.17_spmd} | conditional | flops 552356352 | bytes 35560612 | solution.py:85
  473.1 5.8 dynamic_update_slice.31
  482.2 15.7 %conditional.8 = ((f32[1024,1,4]{0,2,1:T(4,128)S(1)}, f32[1024,1,4]{0,2,1:T(4,128)S(1)}, f32[1024,1,4,128]{0,3,2,1:T(8,128)})) conditional(s32[]{:T(128)} %bitcast.211, (f32[1024,1,4]{0,2,1:T(4,128)S(1)}, f32[1024,1,4]{0,2,1:T(4,128)S(1)}, f32[1024,1,4,128]{0,3,2,1:T(8,128)}) %tuple.165, (s32[]{:T(128)}, f32[1024,1,4]{0,2,1:T(4,128)S(1)}, ...), branch_computations={%region_14.14_spmd, %region_15.17_spmd} | conditional | flops 552356352 | bytes 35560612 | solution.py:85
  492.1 5.8 dynamic_update_slice.31
  501.2 15.7 %conditional.8 = ((f32[1024,1,4]{0,2,1:T(4,128)S(1)}, f32[1024,1,4]{0,2,1:T(4,128)S(1)}, f32[1024,1,4,128]{0,3,2,1:T(8,128)})) conditional(s32[]{:T(128)} %bitcast.211, (f32[1024,1,4]{0,2,1:T(4,128)S(1)}, f32[1024,1,4]{0,2,1:T(4,128)S(1)}, f32[1024,1,4,128]{0,3,2,1:T(8,128)}) %tuple.165, (s32[]{:T(128)}, f32[1024,1,4]{0,2,1:T(4,128)S(1)}, ...), branch_computations={%region_14.14_spmd, %region_15.17_spmd} | conditional | flops 552356352 | bytes 35560612 | solution.py:85
  511.1 5.8 dynamic_update_slice.31
  520.2 15.7 %conditional.8 = ((f32[1024,1,4]{0,2,1:T(4,128)S(1)}, f32[1024,1,4]{0,2,1:T(4,128)S(1)}, f32[1024,1,4,128]{0,3,2,1:T(8,128)})) conditional(s32[]{:T(128)} %bitcast.211, (f32[1024,1,4]{0,2,1:T(4,128)S(1)}, f32[1024,1,4]{0,2,1:T(4,128)S(1)}, f32[1024,1,4,128]{0,3,2,1:T(8,128)}) %tuple.165, (s32[]{:T(128)}, f32[1024,1,4]{0,2,1:T(4,128)S(1)}, ...), branch_computations={%region_14.14_spmd, %region_15.17_spmd} | conditional | flops 552356352 | bytes 35560612 | solution.py:85
  545.9 14.7 %conditional.8 = ((f32[1024,1,4]{0,2,1:T(4,128)S(1)}, f32[1024,1,4]{0,2,1:T(4,128)S(1)}, f32[1024,1,4,128]{0,3,2,1:T(8,128)})) conditional(s32[]{:T(128)} %bitcast.211, (f32[1024,1,4]{0,2,1:T(4,128)S(1)}, f32[1024,1,4]{0,2,1:T(4,128)S(1)}, f32[1024,1,4,128]{0,3,2,1:T(8,128)}) %tuple.165, (s32[]{:T(128)}, f32[1024,1,4]{0,2,1:T(4,128)S(1)}, ...), branch_computations={%region_14.14_spmd, %region_15.17_spmd} | conditional | flops 552356352 | bytes 35560612 | solution.py:85
  563.9 14.7 %conditional.8 = ((f32[1024,1,4]{0,2,1:T(4,128)S(1)}, f32[1024,1,4]{0,2,1:T(4,128)S(1)}, f32[1024,1,4,128]{0,3,2,1:T(8,128)})) conditional(s32[]{:T(128)} %bitcast.211, (f32[1024,1,4]{0,2,1:T(4,128)S(1)}, f32[1024,1,4]{0,2,1:T(4,128)S(1)}, f32[1024,1,4,128]{0,3,2,1:T(8,128)}) %tuple.165, (s32[]{:T(128)}, f32[1024,1,4]{0,2,1:T(4,128)S(1)}, ...), branch_computations={%region_14.14_spmd, %region_15.17_spmd} | conditional | flops 552356352 | bytes 35560612 | solution.py:85
  581.9 14.7 %conditional.8 = ((f32[1024,1,4]{0,2,1:T(4,128)S(1)}, f32[1024,1,4]{0,2,1:T(4,128)S(1)}, f32[1024,1,4,128]{0,3,2,1:T(8,128)})) conditional(s32[]{:T(128)} %bitcast.211, (f32[1024,1,4]{0,2,1:T(4,128)S(1)}, f32[1024,1,4]{0,2,1:T(4,128)S(1)}, f32[1024,1,4,128]{0,3,2,1:T(8,128)}) %tuple.165, (s32[]{:T(128)}, f32[1024,1,4]{0,2,1:T(4,128)S(1)}, ...), branch_computations={%region_14.14_spmd, %region_15.17_spmd} | conditional | flops 552356352 | bytes 35560612 | solution.py:85
  599.9 14.7 %conditional.8 = ((f32[1024,1,4]{0,2,1:T(4,128)S(1)}, f32[1024,1,4]{0,2,1:T(4,128)S(1)}, f32[1024,1,4,128]{0,3,2,1:T(8,128)})) conditional(s32[]{:T(128)} %bitcast.211, (f32[1024,1,4]{0,2,1:T(4,128)S(1)}, f32[1024,1,4]{0,2,1:T(4,128)S(1)}, f32[1024,1,4,128]{0,3,2,1:T(8,128)}) %tuple.165, (s32[]{:T(128)}, f32[1024,1,4]{0,2,1:T(4,128)S(1)}, ...), branch_computations={%region_14.14_spmd, %region_15.17_spmd} | conditional | flops 552356352 | bytes 35560612 | solution.py:85
  617.9 14.7 %conditional.8 = ((f32[1024,1,4]{0,2,1:T(4,128)S(1)}, f32[1024,1,4]{0,2,1:T(4,128)S(1)}, f32[1024,1,4,128]{0,3,2,1:T(8,128)})) conditional(s32[]{:T(128)} %bitcast.211, (f32[1024,1,4]{0,2,1:T(4,128)S(1)}, f32[1024,1,4]{0,2,1:T(4,128)S(1)}, f32[1024,1,4,128]{0,3,2,1:T(8,128)}) %tuple.165, (s32[]{:T(128)}, f32[1024,1,4]{0,2,1:T(4,128)S(1)}, ...), branch_computations={%region_14.14_spmd, %region_15.17_spmd} | conditional | flops 552356352 | bytes 35560612 | solution.py:85
  635.0 6.3 fusion.69
  641.4 304.4 %psum.7 = f32[32]{0:T(128)S(1)} all-reduce(f32[32]{0:T(128)S(1)} %multiply_dynamic-update-slice_fusion), channel_id=1, replica_groups=mesh['dp'=2,'head'=8,'ctx'=16] {'dp','head','ctx'}, use_global_device_ids=true, to_apply=%region_20.21 | all-reduce | flops 32 | bytes 256 | tf_op jit(solution)/shard_map/psum | solution.py:198
  (557 shorter events, 266.0 us)
Async XLA Ops:
  7.7 22.1 %copy-start.3 = (s32[4]{0:T(128)S(1)}, s32[4]{0:T(128)}, u32[]{:S(2)}) copy-start(s32[4]{0:T(128)} %param.22) | copy-start | bytes 52
  7.7 22.3 %copy-start.4 = (f32[4]{0:T(128)S(1)}, f32[4]{0:T(128)}, u32[]{:S(2)}) copy-start(f32[4]{0:T(128)} %param.21) | copy-start | bytes 52
  7.7 22.3 %copy-start.2 = (bf16[1,1024,4,128]{3,2,1,0:T(4,128)(2,1)S(1)}, bf16[1,1024,4,128]{3,2,1,0:T(4,128)(2,1)}, u32[]{:S(2)}) copy-start(bf16[1,1024,4,128]{3,2,1,0:T(4,128)(2,1)} %param.18) | copy-start | bytes 3145732
  7.7 238.8 %all-to-all-start = ((bf16[16,2,1024,1,128]{4,2,3,1,0:T(8,128)(2,1)}), bf16[16,2,1024,1,128]{4,2,3,1,0:T(8,128)(2,1)}, u32[]{:S(2)}, u32[]{:S(2)}) async-start(bf16[16,2,1024,1,128]{4,2,3,1,0:T(8,128)(2,1)} %stack.8), calls=%async_computation | async-start | bytes 16777216 | tf_op jit(solution)/shard_map/all_to_all | solution.py:141
  19.7 201.8 %collective-permute-start.1 = (bf16[2,1024,1,128]{3,1,2,0:T(8,128)(2,1)S(1)}, bf16[2,1024,1,128]{3,1,2,0:T(8,128)(2,1)S(1)}, u32[]{:S(2)}, u32[]{:S(2)}) collective-permute-start(bf16[2,1024,1,128]{3,1,2,0:T(8,128)(2,1)S(1)} %constant_dynamic-update-slice_fusion.1), channel_id=1, source_target_pairs={{0,1},{1,2},{2,3},{3,4},{4,5},{5,6},{6,7},{7,8},{8,9},{9,10},{10,1... | collective-permute-start | bytes 1572872 | tf_op jit(solution)/shard_map/ppermute | solution.py:15
  23.8 219.4 %collective-permute-start = (bf16[2,1024,1,128]{3,1,2,0:T(8,128)(2,1)S(1)}, bf16[2,1024,1,128]{3,1,2,0:T(8,128)(2,1)}, u32[]{:S(2)}, u32[]{:S(2)}) collective-permute-start(bf16[2,1024,1,128]{3,1,2,0:T(8,128)(2,1)S(1)} %constant_dynamic-update-slice_fusion.1), channel_id=1, source_target_pairs={{0,2},{1,3},{2,4},{3,5},{4,6},{5,7},{6,8},{7,9},{8,10},{9,11},{10,... | collective-permute-start | bytes 1572872 | tf_op jit(solution)/shard_map/ppermute | solution.py:15
  446.5 1.9 copy-start
  465.5 1.9 copy-start
  484.5 1.9 copy-start
  503.5 1.9 copy-start
  522.5 1.9 copy-start
  548.2 1.9 copy-start
  566.2 1.9 copy-start
  584.2 1.9 copy-start
  602.2 1.9 copy-start
  620.2 1.9 copy-start
  632.6 2.3 copy-start.1
